TPU v7x, 512 devices: a whole 4x8x8 slice. The times are simulated.
512 devices in a mesh: depth: 2 (over x_hi), row: 16 (over x_lo, y), col: 16 (over z, core).
Axes of the slice: x: 4 (x_hi: 2, x_lo: 2; x = x_hi * 2 + x_lo), y: 8, z: 8, core: 2. Of those that a mesh axis runs over, the one named last changes fastest.
Arguments:
- tokens: bfloat16 [768, 8192], P(('depth', 'row'), 'col'), may hold values from -6 to 6
- gate_weight: bfloat16 [8192, 14336], P('col', 'row'), may hold values from -0.0625 to 0.0625
- up_weight: bfloat16 [8192, 14336], P('col', 'row'), may hold values from -0.0625 to 0.0625
- down_weight: bfloat16 [14336, 8192], P('row', 'col'), may hold values from -0.046875 to 0.046875
Outputs:
- mixed: bfloat16 [768, 8192], P(('depth', 'row'), 'col')
All inputs are finite; a program needn't handle non-finite values.
Results may differ from a plain program's by a relative error of at most 0.0049.
Values may be sent and summed in bfloat16 or wider, within the bound.
A program may use at most 64 MiB of HBM per device.

v0:
```python
import jax
import jax.numpy as jnp
from jax import lax
from jax.sharding import PartitionSpec as P


def shards(tokens, gate_weight, up_weight, down_weight):
    stacked = jnp.stack((gate_weight, up_weight), 0)
    terms = jnp.einsum(
        "tk,skf->stf",
        lax.all_gather(tokens, "row", axis=0, tiled=True),
        stacked,
        preferred_element_type=jnp.float32,
    )
    sums = lax.psum_scatter(terms, "col", scatter_dimension=1, tiled=True)
    hidden_own = (jax.nn.silu(sums[0]) * sums[1]).astype(jnp.bfloat16)
    down_terms = jnp.dot(
        lax.all_gather(hidden_own, "col", axis=0, tiled=True),
        down_weight,
        preferred_element_type=jnp.float32,
    )
    mixed = lax.psum_scatter(down_terms, "row", scatter_dimension=0, tiled=True)
    return mixed.astype(jnp.bfloat16)


def solution(mesh):
    in_specs = (P(("depth", "row"), "col"), P("col", "row"), P("col", "row"), P("row", "col"))
    out_specs = P(("depth", "row"), "col")
    return jax.shard_map(shards, mesh=mesh, in_specs=in_specs, out_specs=out_specs, check_vma=False)
```

profile of v0, /device:TPU:4, one launch (start us, length us, event | category | flops | bytes accessed | tf_op | source)
XLA Modules:
  0.0 276.8 jit_solution(6016061719459843238)
XLA Ops:
  6.5 0.0 copy-start
  6.5 0.0 copy-start.1
  6.5 0.0 all-reduce.3.cloned.1.call-start
  6.5 1.5 copy.7
  8.1 1.5 copy.8
  9.6 0.0 copy-done.1
  9.6 35.7 %all_gather.6 = bf16[384,512]{1,0:T(8,128)(2,1)S(1)} all-gather(bf16[24,512]{1,0:T(8,128)(2,1)S(1)} %copy-done.1), channel_id=1, replica_groups=mesh['depth'=2,'row'=16,'col'=16] {'row'}, dimensions={0}, use_global_device_ids=true | all-gather | bytes 417792 | tf_op jit(solution)/shard_map/all_gather | solution.py:11
  45.3 2.7 fusion.4
  48.0 5.7 %copy.9 = f32[2,384,896]{2,0,1:T(2,128)} copy(f32[2,384,896]{1,2,0:T(8,128)} %fusion.4) | data formatting | bytes 5505024 | tf_op jit(solution)/shard_map/tk,skf->stf/transpose | solution.py:9
  53.7 0.0 all-reduce.3.cloned.1.call-update
  53.7 0.0 reduce-scatter.2.cloned.1.call-start
  53.7 1.3 dynamic-slice
  55.7 121.0 %all-reduce.3.cloned.1.call-done = f32[2,384,896]{2,0,1:T(2,128)} async-done(((f32[2,384,896]{2,0,1:T(2,128)}), f32[2,384,896]{2,0,1:T(2,128)}) %all-reduce.3.cloned.1.call-update) | async-done | bytes 2752528
  176.6 1.1 constant_dynamic-slice_fusion
  177.8 16.8 %all_gather.7 = bf16[384,896]{1,0:T(8,128)(2,1)S(1)} all-gather(bf16[24,896]{1,0:T(8,128)(2,1)S(1)} %fusion.8), channel_id=1, replica_groups=mesh['depth'=2,'row'=16,'col'=16] {'col'}, dimensions={0}, use_global_device_ids=true | all-gather | bytes 731136 | tf_op jit(solution)/shard_map/all_gather | solution.py:18
  194.6 0.0 copy-done
  194.6 1.5 fusion.10
  196.1 0.0 reduce-scatter.2.cloned.1.call-update
  196.1 72.5 %reduce-scatter.2.cloned.1.call-done = f32[24,512]{1,0:T(8,128)} async-done(((f32[384,512]{1,0:T(8,128)}), f32[24,512]{1,0:T(8,128)}) %reduce-scatter.2.cloned.1.call-update) | async-done | bytes 49168 | tf_op jit(solution)/shard_map/reduce_scatter | solution.py:22
  268.6 1.4 convert_element_type.7
  (1 shorter events, 0.0 us)
Async XLA Ops:
  6.5 188.1 %copy-start = (bf16[896,512]{1,0:T(8,128)(2,1)S(1)}, bf16[896,512]{1,0:T(8,128)(2,1)}, u32[]{:S(2)}) copy-start(bf16[896,512]{1,0:T(8,128)(2,1)} %param.7) | copy-start | bytes 2752516
  6.5 3.0 %copy-start.1 = (bf16[24,512]{1,0:T(8,128)(2,1)S(1)}, bf16[24,512]{1,0:T(8,128)(2,1)}, u32[]{:S(2)}) copy-start(bf16[24,512]{1,0:T(8,128)(2,1)} %param.4) | copy-start | bytes 73732
  6.5 170.1 %all-reduce.3.cloned.1.call-start = ((), (), s32[]{:S(2)}) async-start(), calls=%async_computation.2 | async-start | bytes 5505024
  53.7 214.9 %reduce-scatter.2.cloned.1.call-start = ((), (), s32[]{:S(2)}) async-start(), calls=%async_computation.1 | async-start | bytes 835584 | tf_op jit(solution)/shard_map/reduce_scatter | solution.py:22
Sparse Core Ops, SparseCore 0:
  53.8 122.7 all-reduce.2
  196.2 72.3 reduce-scatter.1
where the time goes:
time: 277 us
  waiting for transfers between devices  193 us (70%)
  blocking collectives  52.5 us (19%)
  between operations  14.1 us (5%)
  local copies, waits for them, and re-layouts  11.1 us (4%)
  matrix products  4.17 us (2%)
    unnamed x3, waiting for transfers between devices  121 us
    reduce_scatter x1, waiting for transfers between devices, shards(): mixed = lax.psum_scatter(down_terms, 'row', scatter_dimension=0, tiled=True)  72.5 us
    all_gather x1, blocking collectives, shards(): lax.all_gather(tokens, 'row', axis=0, tiled=True)  35.7 us
    all_gather x1, blocking collectives, shards(): lax.all_gather(hidden_own, 'col', axis=0, tiled=True)  16.8 us
    transpose x1, local copies, waits for them, and re-layouts, shards(): jnp.einsum('tk,skf->stf', lax.all_gather(tokens, 'row', axis=0, tiled=Tru...  5.68 us
  transfers between devices with their start and end apart: 2, of which 2 were waited for; matrix products, arithmetic and copies ran while one was open for 0% of the time, Pallas kernels for 0%

commit v1 on v0

v1 whole, which is shorter than its diff:
```python
import functools

import jax
import jax.numpy as jnp
from jax import lax
from jax.experimental import pallas as pl
from jax.experimental.pallas import tpu as pltpu
from jax.sharding import PartitionSpec as P

MESH = pl.DeviceIdType.MESH
NX, NY, NZ, NC = 2, 8, 8, 2
CHUNKS = ((0, 512), (512, 384))
F32, BF16 = jnp.float32, jnp.bfloat16


def kernel(
    tok, gate, up, down, out,
    wg, wu, wd, tok_all, gate_sum, up_sum, send_b0, send_b1, recv_b0, recv_b1, hid0, hid1, part, send_c, recv_c,
    load_sem, wss, wrs, ass, ars, bss, brs, hss, hrs, css, crs,
):
    depth, row, col = lax.axis_index("depth"), lax.axis_index("row"), lax.axis_index("col")
    x, y = row // NY, lax.rem(row, NY)
    z, core = col // NC, lax.rem(col, NC)
    rows, kd = tok.shape
    home = x == core

    def at(xx, yy, zz, cc):
        return (depth, xx * NY + yy, zz * NC + cc)

    def around(v, n, by):
        return lax.rem(v + by, n)

    def remote(src, dst, ss, rs, device):
        return pltpu.make_async_remote_copy(src, dst, ss, rs, device_id=device, device_id_type=MESH)

    mine = pl.ds(pl.multiple_of(core * kd, kd), kd)
    loads = [
        pltpu.make_async_copy(gate, wg.at[mine], load_sem.at[0]),
        pltpu.make_async_copy(up, wu.at[mine], load_sem.at[1]),
        pltpu.make_async_copy(down, wd.at[core], load_sem.at[2]),
    ]
    for copy in loads:
        copy.start()

    barrier = pltpu.get_barrier_semaphore()

    def greet(device):
        pl.semaphore_signal(barrier, inc=1, device_id=device, device_id_type=MESH)

    def greet_row(i, c):
        dx, dy = i // NY, lax.rem(i, NY)
        for device in (
            at(around(x, NX, dx), around(y, NY, dy), z, x),
            at(core, around(y, NY, dy), z, around(core, NC, dx)),
        ):
            @pl.when(jnp.logical_not(jnp.logical_and(home, i == 0)))
            def _():
                greet(device)

        return c

    lax.fori_loop(0, NX * NY, greet_row, 0)

    def greet_col(i, c):
        greet(at(x, y, around(z, NZ, i), core))
        return c

    lax.fori_loop(1, NZ, greet_col, 0)
    greet(at(x, y, z, 1 - core))
    pl.semaphore_wait(barrier, 2 * NX * NY + NZ - jnp.where(home, 2, 0))

    def tok_copy(i):
        dx, dy = i // NY, lax.rem(i, NY)
        return remote(
            tok, tok_all.at[y, core], ass.at[i], ars.at[y, core], at(around(x, NX, dx), around(y, NY, dy), z, x)
        )

    def tok_send(i, c):
        own = jnp.logical_and(home, i == 0)

        @pl.when(own)
        def _():
            pltpu.make_async_copy(tok, tok_all.at[y, core], ars.at[y, core]).start()

        @pl.when(jnp.logical_not(own))
        def _():
            tok_copy(i).start()

        return c

    lax.fori_loop(0, NX * NY, tok_send, 0)

    other = at(x, y, z, 1 - core)
    swaps = [
        remote(gate, wg.at[mine], wss.at[0], wrs.at[0], other),
        remote(up, wu.at[mine], wss.at[1], wrs.at[1], other),
        remote(down, wd.at[core], wss.at[2], wrs.at[2], other),
    ]
    for copy in swaps:
        copy.start()

    def tok_wait(i, c):
        yy, cc = i // NC, lax.rem(i, NC)
        pltpu.make_async_copy(tok, tok_all.at[yy, cc], ars.at[yy, cc]).wait()
        return c

    lax.fori_loop(0, NY * NC, tok_wait, 0)
    loads[0].wait()
    swaps[0].wait_recv()
    loads[1].wait()
    swaps[1].wait_recv()

    lhs = jnp.concatenate(
        [tok_all[:, cc].astype(F32).reshape(NY * rows, kd).astype(BF16) for cc in range(NC)], axis=1
    )

    send_b, recv_b, hid = (send_b0, send_b1), (recv_b0, recv_b1), (hid0, hid1)

    def sum_copy(ch, i):
        return remote(
            send_b[ch].at[i - 1], recv_b[ch].at[i - 1], bss.at[ch, i - 1], brs.at[ch, i - 1],
            at(x, y, around(z, NZ, i), core),
        )

    def hid_copy(ch, i):
        return remote(
            hid[ch].at[z], hid[ch].at[z], hss.at[ch, i - 1], hrs.at[ch, i - 1], at(x, y, around(z, NZ, i), core)
        )

    def own_rows(zz):
        return pl.ds(pl.multiple_of(zz * rows, 8), rows)

    for ch, (lo, width) in enumerate(CHUNKS):
        cols = pl.ds(lo, width)
        gate_sum[:, cols] = jnp.dot(lhs, wg[:, cols], preferred_element_type=F32)
        up_sum[:, cols] = jnp.dot(lhs, wu[:, cols], preferred_element_type=F32)

        def sum_send(i, c):
            there = own_rows(around(z, NZ, i))
            both = jnp.concatenate([gate_sum[there, cols], up_sum[there, cols]], axis=0)
            send_b[ch][i - 1] = both.astype(BF16)
            sum_copy(ch, i).start()
            return c

        lax.fori_loop(1, NZ, sum_send, 0)

    for ch, (lo, width) in enumerate(CHUNKS):
        cols = pl.ds(lo, width)
        both = jnp.concatenate([gate_sum[own_rows(z), cols], up_sum[own_rows(z), cols]], axis=0)
        for i in range(1, NZ):
            sum_copy(ch, i).wait_recv()
            both = both + recv_b[ch][i - 1].astype(F32)
        hid[ch][z] = (jax.nn.silu(both[:rows]) * both[rows:]).astype(BF16)

        def hid_send(i, c):
            hid_copy(ch, i).start()
            return c

        lax.fori_loop(1, NZ, hid_send, 0)

    loads[2].wait()
    swaps[2].wait_recv()
    for ch, (lo, width) in enumerate(CHUNKS):
        for i in range(1, NZ):
            back = around(z, NZ, NZ - i)
            remote(
                hid[ch].at[back], hid[ch].at[back], hss.at[ch, i - 1], hrs.at[ch, i - 1], at(x, y, back, core)
            ).wait_recv()
        h = hid[ch][...].astype(F32).reshape(NZ * rows, width).astype(BF16)
        for cc in range(NC):
            term = jnp.dot(h, wd[cc, lo : lo + width], preferred_element_type=F32)
            part[cc] = term if ch == 0 else part[cc] + term

    def out_copy(i):
        dc, dy = i // NY, lax.rem(i, NY)
        return remote(
            send_c.at[i], recv_c.at[row], css.at[i], crs.at[row], at(core, around(y, NY, dy), z, around(core, NC, dc))
        )

    def out_send(i, c):
        dc, dy = i // NY, lax.rem(i, NY)
        send_c[i] = part[around(core, NC, dc), own_rows(around(y, NY, dy))].astype(BF16)
        own = jnp.logical_and(home, i == 0)

        @pl.when(own)
        def _():
            pltpu.make_async_copy(send_c.at[i], recv_c.at[row], crs.at[row]).start()

        @pl.when(jnp.logical_not(own))
        def _():
            out_copy(i).start()

        return c

    lax.fori_loop(0, NC * NY, out_send, 0)

    total = jnp.zeros(out.shape, F32)
    for i in range(NX * NY):
        pltpu.make_async_copy(send_c.at[0], recv_c.at[i], crs.at[i]).wait()
        total = total + recv_c[i].astype(F32)
    out[...] = total.astype(BF16)

    for copy in swaps:
        copy.wait_send()

    def row_sent(i, c):
        @pl.when(jnp.logical_not(jnp.logical_and(home, i == 0)))
        def _():
            tok_copy(i).wait_send()
            out_copy(i).wait_send()

        return c

    lax.fori_loop(0, NX * NY, row_sent, 0)
    for ch in range(len(CHUNKS)):

        def col_sent(i, c):
            sum_copy(ch, i).wait_send()
            hid_copy(ch, i).wait_send()
            return c

        lax.fori_loop(1, NZ, col_sent, 0)


def shards(tokens, gate_weight, up_weight, down_weight):
    rows, kd = tokens.shape
    ff, nd = down_weight.shape
    tall = NY * rows
    widths = [w for _, w in CHUNKS]
    dma = pltpu.SemaphoreType.DMA
    n = len(CHUNKS)
    return pl.pallas_call(
        kernel,
        out_shape=jax.ShapeDtypeStruct((rows, nd), BF16),
        in_specs=[pl.BlockSpec(memory_space=pl.ANY)] * 4,
        out_specs=pl.BlockSpec(memory_space=pltpu.VMEM),
        scratch_shapes=[
            pltpu.VMEM((NC * kd, ff), BF16),
            pltpu.VMEM((NC * kd, ff), BF16),
            pltpu.VMEM((NC, ff, nd), BF16),
            pltpu.VMEM((NY, NC, rows, kd), BF16),
            pltpu.VMEM((tall, ff), F32),
            pltpu.VMEM((tall, ff), F32),
            *[pltpu.VMEM((NZ - 1, 2 * rows, w), BF16) for w in widths],
            *[pltpu.VMEM((NZ - 1, 2 * rows, w), BF16) for w in widths],
            *[pltpu.VMEM((NZ, rows, w), BF16) for w in widths],
            pltpu.VMEM((NC, tall, nd), F32),
            pltpu.VMEM((NC * NY, rows, nd), BF16),
            pltpu.VMEM((NX * NY, rows, nd), BF16),
            dma((3,)), dma((3,)), dma((3,)),
            dma((NX * NY,)), dma((NY, NC)),
            dma((n, NZ - 1)), dma((n, NZ - 1)), dma((n, NZ - 1)), dma((n, NZ - 1)),
            dma((NC * NY,)), dma((NX * NY,)),
        ],
        compiler_params=pltpu.CompilerParams(collective_id=0, has_side_effects=True, vmem_limit_bytes=60 << 20),
        name="feed_forward",
    )(tokens, gate_weight, up_weight, down_weight)


def solution(mesh):
    in_specs = (P(("depth", "row"), "col"), P("col", "row"), P("col", "row"), P("row", "col"))
    out_specs = P(("depth", "row"), "col")
    return jax.shard_map(shards, mesh=mesh, in_specs=in_specs, out_specs=out_specs, check_vma=False)
```

time: 277 us -> 63.5 us (0.23)
  the two profiles are of different devices: /device:TPU:4 before, /device:TPU:1 now
where the time goes in v1:
time: 63.5 us; the launch traced here: 62.7 us
  Pallas kernels  61.4 us (97%)
  local copies, waits for them, and re-layouts  1.35 us (2%)
    pallas_call x1, Pallas kernels, shards(): pl.pallas_call(kernel, out_shape=jax.ShapeDtypeStruct((rows, nd), BF16),...  61.4 us
    unnamed x1, local copies, waits for them, and re-layouts  1.35 us

profile of v1, /device:TPU:1, one launch (start us, length us, event | category | flops | bytes accessed | tf_op | source)
XLA Modules:
  0.0 62.7 jit_solution(3653494446447532191)
XLA Ops:
  0.0 61.4 %feed_forward.1 = bf16[24,512]{1,0:T(8,128)(2,1)} custom-call(bf16[24,512]{1,0:T(8,128)(2,1)} %tok.1, bf16[512,896]{1,0:T(8,128)(2,1)} %gate.1, bf16[512,896]{1,0:T(8,128)(2,1)} %up.1, bf16[896,512]{1,0:T(8,128)(2,1)} %down.1), custom_call_target="tpu_custom_call" | custom-call | tf_op jit(solution)/shard_map/feed_forward/pallas_call | solution.py:232
  61.4 1.3 %copy.6 = bf16[24,512]{1,0:T(8,128)(2,1)} copy(bf16[24,512]{1,0:T(8,128)(2,1)} %feed_forward.1) | data formatting | bytes 49152

commit v2 on v0

v2 whole, which is shorter than its diff:
```python
import jax
import jax.numpy as jnp
from jax import lax
from jax.experimental import pallas as pl
from jax.experimental.pallas import tpu as pltpu
from jax.sharding import PartitionSpec as P

MESH = pl.DeviceIdType.MESH
NX, NY, NZ, NC = 2, 8, 8, 2
NG = NX * NY
FAR = (4, 3, 5, 2, 6, 1, 7, 0)
TILE = 8
F32, BF16 = jnp.float32, jnp.bfloat16


def fold(v):
    half = v.shape[1] // 2
    return jnp.concatenate([v[:, :half], v[:, half:]], axis=0).astype(BF16)


def kernel(
    tok, gate, up, down, out,
    tok_in, wg, wu, wd, tok_own, tok_first, tok_rest, gate_sum, up_sum, send_b, recv_b, hid, part, send_c, recv_c,
    load_sem, wss, wrs, ass, ars, rss, rrs, fss, frs, bss, brs, hss, hrs, css, crs,
):
    depth, row, col = lax.axis_index("depth"), lax.axis_index("row"), lax.axis_index("col")
    x, y = row // NY, lax.rem(row, NY)
    z, core = col // NC, lax.rem(col, NC)
    rows, kd = tok.shape
    ff = gate.shape[1]
    chunks = rows // TILE
    home = x == core

    def at(xx, yy, zz, cc):
        return (depth, xx * NY + yy, zz * NC + cc)

    def around(v, n, by):
        return lax.rem(v + by, n)

    def zat(i):
        return lax.rem(z + NZ + jnp.where(core == 0, i, -i), NZ)

    def remote(src, dst, ss, rs, device):
        return pltpu.make_async_remote_copy(src, dst, ss, rs, device_id=device, device_id_type=MESH)

    def rows_of(i):
        return pl.ds(pl.multiple_of(i * TILE, TILE), TILE)

    mine = pl.ds(pl.multiple_of(core * kd, kd), kd)
    tok_load = pltpu.make_async_copy(tok, tok_in, load_sem.at[3])
    tok_load.start()
    loads = [
        pltpu.make_async_copy(gate, wg.at[mine], load_sem.at[0]),
        pltpu.make_async_copy(up, wu.at[mine], load_sem.at[1]),
        pltpu.make_async_copy(down, wd.at[core], load_sem.at[2]),
    ]
    for copy in loads:
        copy.start()

    barrier = pltpu.get_barrier_semaphore()

    def greet(device):
        pl.semaphore_signal(barrier, inc=1, device_id=device, device_id_type=MESH)

    for dy in FAR:
        yy = around(y, NY, dy)
        greet(at(1 - core, yy, z, x))
        greet(at(core, yy, z, 1 - x))
        if dy:
            greet(at(core, yy, z, x))
        else:

            @pl.when(jnp.logical_not(home))
            def _():
                greet(at(core, yy, z, x))

    for i in range(1, NZ):
        greet(at(x, y, around(z, NZ, i), core))
    other = at(x, y, z, 1 - core)
    tok_load.wait()
    for t in range(chunks):
        tok_own[t] = fold(tok_in[...].astype(F32)[t * TILE : (t + 1) * TILE])
    pl.semaphore_wait(barrier, 3 * NY + NZ - 1 - jnp.where(home, 1, 0))

    def first_copy(i):
        dx, dy = i // NY, lax.rem(i, NY)
        there = at(around(x, NX, dx), around(y, NY, dy), z, x)
        return remote(tok_own.at[0], tok_first.at[y, core], ass.at[i], ars.at[y, core], there)

    def rest_copy(dy):
        there = at(x, around(y, NY, dy), z, x)
        return remote(tok_own.at[1:], tok_rest.at[y, core], rss.at[dy], rrs.at[y, core], there)

    def forward_copy(yy):
        return remote(tok_rest.at[yy], tok_rest.at[yy], fss.at[yy], frs.at[yy], at(1 - x, y, z, core))

    def start_unless_own(dy, dx, copy, src, dst, sem):
        if dy or dx:
            copy.start()
            return

        @pl.when(home)
        def _():
            pltpu.make_async_copy(src, dst, sem).start()

        @pl.when(jnp.logical_not(home))
        def _():
            copy.start()

    swaps = [
        remote(gate, wg.at[mine], wss.at[0], wrs.at[0], other),
        remote(up, wu.at[mine], wss.at[1], wrs.at[1], other),
        remote(down, wd.at[core], wss.at[2], wrs.at[2], other),
    ]
    for dy in FAR:
        for dx in (1, 0):
            start_unless_own(
                dy, dx, first_copy(dx * NY + dy), tok_own.at[0], tok_first.at[y, core], ars.at[y, core]
            )
    for copy in swaps:
        copy.start()
    for dy in FAR:
        start_unless_own(dy, 0, rest_copy(dy), tok_own.at[1:], tok_rest.at[y, core], rrs.at[y, core])

    def forward():
        @pl.when(home)
        def _():
            for dy in reversed(FAR):
                yy = around(y, NY, dy)
                for cc in range(NC):
                    pltpu.make_async_copy(tok_own.at[1:], tok_rest.at[yy, cc], rrs.at[yy, cc]).wait()
                forward_copy(yy).start()

    def rest_wait():
        @pl.when(jnp.logical_not(home))
        def _():
            for yy in range(NY):
                forward_copy(yy).wait_recv()

    first = ((-1, -4), (-1, -2), (1, 3), (1, 1))
    then = ((-3, -3), (-1, -1), (2, 2))

    def sum_copy(t, j):
        step = (first + then)[j][0]
        return remote(
            send_b.at[t, j], recv_b.at[t, j], bss.at[t, j], brs.at[t, j], at(x, y, zat(step), core)
        )

    def own_part(t, who):
        there = rows_of(who)
        return jnp.concatenate([gate_sum[t, there], up_sum[t, there]], axis=0)

    def up_products(t):
        if t == 0:
            for yy in range(NY):
                for cc in range(NC):
                    pltpu.make_async_copy(tok_own.at[0], tok_first.at[yy, cc], ars.at[yy, cc]).wait()
            loads[0].wait()
            swaps[0].wait_recv()
            loads[1].wait()
            swaps[1].wait_recv()
        blocks = []
        for cc in range(NC):
            v = (tok_first[:, cc] if t == 0 else tok_rest[:, cc, t - 1]).astype(F32)
            blocks += [v[:, :TILE].reshape(NY * TILE, kd // 2), v[:, TILE:].reshape(NY * TILE, kd // 2)]
        lhs = jnp.concatenate(blocks, axis=1).astype(BF16)
        gate_sum[t] = jnp.dot(lhs, wg[...], preferred_element_type=F32)
        up_sum[t] = jnp.dot(lhs, wu[...], preferred_element_type=F32)
        for j, (_, who) in enumerate(first):
            send_b[t, j] = own_part(t, zat(who)).astype(BF16)
            sum_copy(t, j).start()

    def add_on_way(t):
        for k, (_, who) in enumerate(then):
            j = len(first) + k
            sum_copy(t, k).wait_recv()
            send_b[t, j] = (own_part(t, zat(who)) + recv_b[t, k].astype(F32)).astype(BF16)
            sum_copy(t, j).start()

    spread = ((3, 0), (1, 0), (-2, 0), (-1, 0))
    onward = ((1, -3), (1, -1), (-1, 2))

    def hid_copy(t, j):
        step, whose = (spread + onward)[j]
        block = hid.at[t, zat(whose)]
        return remote(block, block, hss.at[t, j], hrs.at[t, j], at(x, y, zat(step), core))

    def hid_arrived(t, j):
        step, whose = (spread + onward)[j]
        block = hid.at[t, zat(whose - step)]
        remote(block, block, hss.at[t, j], hrs.at[t, j], at(x, y, zat(step), core)).wait_recv()

    def hidden(t):
        both = own_part(t, z)
        for j in range(len(first) - 1, len(first) + len(then)):
            sum_copy(t, j).wait_recv()
            both = both + recv_b[t, j].astype(F32)
        h = jax.nn.silu(both[:TILE]) * both[TILE:]
        wide = hid.shape[3]
        right = jnp.concatenate([h[:, wide:], jnp.zeros((TILE, 2 * wide - ff), F32)], axis=1)
        hid[t, z] = jnp.concatenate([h[:, :wide], right], axis=0).astype(BF16)
        for j in range(len(spread)):
            hid_copy(t, j).start()

    def pass_on(t):
        for k in range(len(onward)):
            hid_arrived(t, k)
            hid_copy(t, len(spread) + k).start()

    def out_copy(t, i):
        dc, dy = i // NY, lax.rem(i, NY)
        there = at(core, around(y, NY, dy), z, around(core, NC, dc))
        return remote(send_c.at[t, i], recv_c.at[t, row], css.at[t, i], crs.at[t, row], there)

    def down_products(t):
        for j in range(len(spread) - 1, len(spread) + len(onward)):
            hid_arrived(t, j)
        if t == 0:
            loads[2].wait()
            swaps[2].wait_recv()
        v, wide = hid[t].astype(F32), hid.shape[3]
        left, right = v[:, :TILE].reshape(NZ * TILE, wide), v[:, TILE:].reshape(NZ * TILE, wide)
        h = jnp.concatenate([left, right[:, : ff - wide]], axis=1).astype(BF16)
        for cc in range(NC):
            part[cc] = jnp.dot(h, wd[cc], preferred_element_type=F32)

        for dy in FAR:
            for dc in (1, 0):
                i = dc * NY + dy
                send_c[t, i] = fold(part[around(core, NC, dc), rows_of(around(y, NY, dy))])
                start_unless_own(dy, dc, out_copy(t, i), send_c.at[t, i], recv_c.at[t, row], crs.at[t, row])

    def out_rows(t):
        total = jnp.zeros((2 * TILE, kd // 2), F32)
        for i in range(NG):
            pltpu.make_async_copy(send_c.at[t, 0], recv_c.at[t, i], crs.at[t, i]).wait()
            total = total + recv_c[t, i].astype(F32)
        return jnp.concatenate([total[:TILE], total[TILE:]], axis=1)

    def unless_own(copies):
        @pl.when(jnp.logical_not(home))
        def _():
            copies[0].wait_send()

        for copy in copies[1:]:
            copy.wait_send()

    up_products(0)
    forward()
    add_on_way(0)
    rest_wait()
    up_products(1)
    up_products(2)
    hidden(0)
    add_on_way(1)
    add_on_way(2)
    pass_on(0)
    hidden(1)
    hidden(2)
    down_products(0)
    pass_on(1)
    pass_on(2)
    down_products(1)
    down_products(2)

    for copy in swaps:
        copy.wait_send()
    unless_own([first_copy(i) for i in range(NG)])
    unless_own([rest_copy(dy) for dy in range(NY)])

    @pl.when(home)
    def _():
        for yy in range(NY):
            forward_copy(yy).wait_send()

    for t in range(chunks):
        for j in range(NZ - 1):
            sum_copy(t, j).wait_send()
            hid_copy(t, j).wait_send()
    blocks = []
    for t in range(chunks):
        unless_own([out_copy(t, i) for i in range(NG)])
        blocks.append(out_rows(t))
    out[...] = jnp.concatenate(blocks, axis=0).astype(BF16)


def shards(tokens, gate_weight, up_weight, down_weight):
    rows, kd = tokens.shape
    ff, nd = down_weight.shape
    n, tall = rows // TILE, NY * TILE
    wide = 512
    dma = pltpu.SemaphoreType.DMA
    return pl.pallas_call(
        kernel,
        out_shape=pltpu.VMEM((rows, nd), BF16),
        in_specs=[pl.BlockSpec(memory_space=pl.ANY)] * 4,
        out_specs=pl.BlockSpec(memory_space=pltpu.VMEM),
        scratch_shapes=[
            pltpu.VMEM((rows, kd), BF16),
            pltpu.VMEM((NC * kd, ff), BF16),
            pltpu.VMEM((NC * kd, ff), BF16),
            pltpu.VMEM((NC, ff, nd), BF16),
            pltpu.VMEM((n, 2 * TILE, kd // 2), BF16),
            pltpu.VMEM((NY, NC, 2 * TILE, kd // 2), BF16),
            pltpu.VMEM((NY, NC, n - 1, 2 * TILE, kd // 2), BF16),
            pltpu.VMEM((n, tall, ff), F32),
            pltpu.VMEM((n, tall, ff), F32),
            pltpu.VMEM((n, NZ - 1, 2 * TILE, ff), BF16),
            pltpu.VMEM((n, NZ - 1, 2 * TILE, ff), BF16),
            pltpu.VMEM((n, NZ, 2 * TILE, wide), BF16),
            pltpu.VMEM((NC, tall, nd), F32),
            pltpu.VMEM((n, NG, 2 * TILE, nd // 2), BF16),
            pltpu.VMEM((n, NG, 2 * TILE, nd // 2), BF16),
            dma((4,)), dma((3,)), dma((3,)),
            dma((NG,)), dma((NY, NC)), dma((NY,)), dma((NY, NC)), dma((NY,)), dma((NY,)),
            dma((n, NZ - 1)), dma((n, NZ - 1)), dma((n, NZ - 1)), dma((n, NZ - 1)),
            dma((n, NG)), dma((n, NG)),
        ],
        compiler_params=pltpu.CompilerParams(collective_id=0, has_side_effects=True, vmem_limit_bytes=60 << 20),
        name="feed_forward",
    )(tokens, gate_weight, up_weight, down_weight)


def solution(mesh):
    in_specs = (P(("depth", "row"), "col"), P("col", "row"), P("col", "row"), P("row", "col"))
    out_specs = P(("depth", "row"), "col")
    return jax.shard_map(shards, mesh=mesh, in_specs=in_specs, out_specs=out_specs, check_vma=False)
```

time: 277 us -> 54.6 us (0.20)
  the two profiles are of different devices: /device:TPU:4 before, /device:TPU:1 now
where the time goes in v2:
time: 54.6 us; the launch traced here: 54.4 us
  Pallas kernels  53.8 us (99%)
  local copies, waits for them, and re-layouts  0.61 us (1%)
    pallas_call x1, Pallas kernels, shards(): pl.pallas_call(kernel, out_shape=pltpu.VMEM((rows, nd), BF16), in_specs=[...  53.8 us

profile of v2, /device:TPU:1, one launch (start us, length us, event | category | flops | bytes accessed | tf_op | source)
XLA Modules:
  0.0 54.4 jit_solution(3358812345681704987)
XLA Ops:
  0.0 53.8 %feed_forward.1 = bf16[24,512]{1,0:T(8,128)(2,1)S(1)} custom-call(bf16[24,512]{1,0:T(8,128)(2,1)} %tok.1, bf16[512,896]{1,0:T(8,128)(2,1)} %gate.1, bf16[512,896]{1,0:T(8,128)(2,1)} %up.1, bf16[896,512]{1,0:T(8,128)(2,1)} %down.1), custom_call_target="tpu_custom_call" | custom-call | tf_op jit(solution)/shard_map/feed_forward/pallas_call | solution.py:293
  53.8 0.6 %copy.6 = bf16[24,512]{1,0:T(8,128)(2,1)} copy(bf16[24,512]{1,0:T(8,128)(2,1)S(1)} %feed_forward.1) | data formatting | bytes 49152

commit v3 on v2

v3 whole, which is shorter than its diff:
```python
import jax
import jax.numpy as jnp
from jax import lax
from jax.experimental import pallas as pl
from jax.experimental.pallas import tpu as pltpu
from jax.sharding import PartitionSpec as P

MESH = pl.DeviceIdType.MESH
NX, NY, NZ, NC = 2, 8, 8, 2
NG = NX * NY
CHUNKS = (
    ((0, 0, 3), (1, 0, 3), (7, 0, 2)),
    ((4, 0, 3), (3, 0, 3), (5, 0, 2)),
    ((7, 2, 1), (5, 2, 1), (2, 0, 3), (6, 0, 3)),
)
DIRECT = tuple((i, i) for i in (4, -3, 3, -2, 2, -1, 1))
SUM_TREE = (((-1, -4), (-1, -2), (1, 3), (1, 1)), ((-3, -3), (-1, -1), (2, 2)))
SUMS = ((DIRECT, ()), SUM_TREE, SUM_TREE)
SPREAD = tuple((i, 0) for i in (4, -3, 3, -2, 2, -1, 1))
HID_TREE = (((3, 0), (1, 0), (-2, 0), (-1, 0)), ((1, -3), (1, -1), (-1, 2)))
HIDS = ((SPREAD, ()), (SPREAD, ()), (SPREAD, ()))
ORDER = tuple(o for chunk in CHUNKS for o, tile, _ in chunk if tile == 0)
TILE = 8
F32, BF16 = jnp.float32, jnp.bfloat16


def fold(v):
    half = v.shape[1] // 2
    v = v.reshape(-1, TILE, 2 * half)
    return jnp.concatenate([v[:, :, :half], v[:, :, half:]], axis=1).astype(BF16)


def kernel(
    tok, gate, up, down, out,
    tok_in, wg, wu, wd, tok_own, tok_all, gate_sum, up_sum, send_b, recv_b, hid, part, send_c, recv_c,
    load_sem, wss, wrs, ass, ars, fss, frs, bss, brs, hss, hrs, css, crs,
):
    depth, row, col = lax.axis_index("depth"), lax.axis_index("row"), lax.axis_index("col")
    x, y = row // NY, lax.rem(row, NY)
    z, core = col // NC, lax.rem(col, NC)
    rows, kd = tok.shape
    ff = gate.shape[1]
    tiles, chunks = rows // TILE, len(CHUNKS)
    home = x == core

    def at(xx, yy, zz, cc):
        return (depth, xx * NY + yy, zz * NC + cc)

    def around(v, n, by):
        return lax.rem(v + by, n)

    def zat(i):
        return lax.rem(z + NZ + jnp.where(core == 0, i, -i), NZ)

    def remote(src, dst, ss, rs, device):
        return pltpu.make_async_remote_copy(src, dst, ss, rs, device_id=device, device_id_type=MESH)

    def rows_of(i):
        return pl.ds(pl.multiple_of(i * TILE, TILE), TILE)

    mine = pl.ds(pl.multiple_of(core * kd, kd), kd)
    tok_load = pltpu.make_async_copy(tok, tok_in, load_sem.at[3])
    tok_load.start()
    loads = [
        pltpu.make_async_copy(gate, wg.at[mine], load_sem.at[0]),
        pltpu.make_async_copy(up, wu.at[mine], load_sem.at[1]),
        pltpu.make_async_copy(down, wd.at[core], load_sem.at[2]),
    ]
    for copy in loads:
        copy.start()

    barrier = pltpu.get_barrier_semaphore()

    def greet(device):
        pl.semaphore_signal(barrier, inc=1, device_id=device, device_id_type=MESH)

    for o in ORDER:
        yy = around(y, NY, o)
        greet(at(1 - core, yy, z, x))
        greet(at(core, yy, z, 1 - x))
        if o:
            greet(at(core, yy, z, x))
        else:

            @pl.when(jnp.logical_not(home))
            def _():
                greet(at(core, yy, z, x))

    for i in range(1, NZ):
        greet(at(x, y, around(z, NZ, i), core))
    other = at(x, y, z, 1 - core)
    tok_load.wait()
    tok_own[...] = fold(tok_in[...].astype(F32))
    pl.semaphore_wait(barrier, 3 * NY + NZ - 1 - jnp.where(home, 1, 0))

    def tok_copy(o, dx):
        there = at(around(x, NX, dx), around(y, NY, NY - o), z, x)
        return remote(tok_own, tok_all.at[y, core], ass.at[dx, o], ars.at[y, core], there)

    def tok_sends(t):
        for o, tile, _ in CHUNKS[t]:
            for dx in (1, 0) if t == 0 else (0,):
                if tile == 0:
                    start_unless_own(o, dx, tok_copy(o, dx), tok_own, tok_all.at[y, core], ars.at[y, core])

    def forward_copy(yy):
        return remote(tok_all.at[yy], tok_all.at[yy], fss.at[yy], frs.at[yy], at(1 - x, y, z, core))

    def tok_wait(yy):
        for cc in range(NC):
            pltpu.make_async_copy(tok_own, tok_all.at[yy, cc], ars.at[yy, cc]).wait()

    def forward(t):
        @pl.when(home)
        def _():
            for o, tile, _ in CHUNKS[t]:
                if tile == 0:
                    yy = around(y, NY, o)
                    tok_wait(yy)
                    forward_copy(yy).start()

    def start_unless_own(dy, dx, copy, src, dst, sem):
        if dy or dx:
            copy.start()
            return

        @pl.when(home)
        def _():
            pltpu.make_async_copy(src, dst, sem).start()

        @pl.when(jnp.logical_not(home))
        def _():
            copy.start()

    swaps = [
        remote(gate, wg.at[mine], wss.at[0], wrs.at[0], other),
        remote(up, wu.at[mine], wss.at[1], wrs.at[1], other),
        remote(down, wd.at[core], wss.at[2], wrs.at[2], other),
    ]
    tok_sends(0)
    for copy in swaps:
        copy.start()
    for t in range(1, chunks):
        tok_sends(t)

    def sum_copy(t, j):
        step = (SUMS[t][0] + SUMS[t][1])[j][0]
        return remote(
            send_b.at[t, j], recv_b.at[t, j], bss.at[t, j], brs.at[t, j], at(x, y, zat(step), core)
        )

    def own_part(t, who):
        there = rows_of(who)
        return jnp.concatenate([gate_sum[t, there], up_sum[t, there]], axis=0)

    def up_products(t):
        blocks = []
        for o, tile, n in CHUNKS[t]:
            yy = around(y, NY, o)
            if tile == 0:
                if t == 0:
                    tok_wait(yy)
                else:

                    @pl.when(jnp.logical_not(home))
                    def _():
                        forward_copy(yy).wait_recv()

            parts = []
            for cc in range(NC):
                v = tok_all[yy, cc, tile : tile + n].astype(F32)
                parts += [v[:, :TILE].reshape(n * TILE, kd // 2), v[:, TILE:].reshape(n * TILE, kd // 2)]
            blocks.append(jnp.concatenate(parts, axis=1))
        if t == 0:
            loads[0].wait()
            swaps[0].wait_recv()
            loads[1].wait()
            swaps[1].wait_recv()
        lhs = jnp.concatenate(blocks, axis=0).astype(BF16)
        gate_sum[t] = jnp.dot(lhs, wg[...], preferred_element_type=F32)
        up_sum[t] = jnp.dot(lhs, wu[...], preferred_element_type=F32)
        for j, (_, who) in enumerate(SUMS[t][0]):
            send_b[t, j] = own_part(t, zat(who)).astype(BF16)
            sum_copy(t, j).start()

    def add_on_way(t):
        for k, (_, who) in enumerate(SUMS[t][1]):
            j = len(SUMS[t][0]) + k
            sum_copy(t, k).wait_recv()
            send_b[t, j] = (own_part(t, zat(who)) + recv_b[t, k].astype(F32)).astype(BF16)
            sum_copy(t, j).start()

    def hid_copy(t, j):
        step, whose = (HIDS[t][0] + HIDS[t][1])[j]
        block = hid.at[t, zat(whose)]
        return remote(block, block, hss.at[t, j], hrs.at[t, j], at(x, y, zat(step), core))

    def hid_arrived(t, j):
        step, whose = (HIDS[t][0] + HIDS[t][1])[j]
        block = hid.at[t, zat(whose - step)]
        remote(block, block, hss.at[t, j], hrs.at[t, j], at(x, y, zat(step), core)).wait_recv()

    def hidden(t):
        both = own_part(t, z)
        for j in range(len(SUMS[t][1]), NZ - 1):
            sum_copy(t, j).wait_recv()
            both = both + recv_b[t, j].astype(F32)
        h = jax.nn.silu(both[:TILE]) * both[TILE:]
        hid[t, z] = h.astype(BF16)
        for j in range(len(HIDS[t][0])):
            hid_copy(t, j).start()

    def pass_on(t):
        for k in range(len(HIDS[t][1])):
            hid_arrived(t, k)
            hid_copy(t, len(HIDS[t][0]) + k).start()

    def out_copy(o, tile, n, dc):
        there = at(core, around(y, NY, o), z, around(core, NC, dc))
        return remote(
            send_c.at[dc, o, tile : tile + n], recv_c.at[row, tile : tile + n],
            css.at[dc, o, tile], crs.at[row, tile], there,
        )

    def down_products(t):
        for j in range(len(HIDS[t][1]), NZ - 1):
            hid_arrived(t, j)
        if t == 0:
            loads[2].wait()
            swaps[2].wait_recv()
        h = hid[t].astype(F32).reshape(NZ * TILE, ff).astype(BF16)
        for cc in range(NC):
            part[cc] = jnp.dot(h, wd[cc], preferred_element_type=F32)

        at_tile = 0
        for o, tile, n in CHUNKS[t]:
            for dc in (1, 0):
                term = part[around(core, NC, dc), at_tile * TILE : (at_tile + n) * TILE]
                send_c[dc, o, tile : tile + n] = fold(term)
                here = pl.ds(tile, n)
                start_unless_own(
                    o, dc, out_copy(o, tile, n, dc), send_c.at[dc, o, here], recv_c.at[row, here],
                    crs.at[row, tile],
                )
            at_tile += n

    def unless_own(copies):
        @pl.when(jnp.logical_not(home))
        def _():
            copies[0].wait_send()

        for copy in copies[1:]:
            copy.wait_send()

    up_products(0)
    forward(1)
    forward(2)
    add_on_way(0)
    up_products(1)
    up_products(2)
    add_on_way(1)
    hidden(0)
    add_on_way(2)
    hidden(1)
    hidden(2)
    down_products(0)
    down_products(1)
    down_products(2)

    for copy in swaps:
        copy.wait_send()
    near = [o for o, _, _ in CHUNKS[0]]
    unless_own([tok_copy(o, dx) for o in range(NY) for dx in range(NX if o in near else 1)])

    @pl.when(home)
    def _():
        for o in ORDER[len(near) :]:
            forward_copy(around(y, NY, o)).wait_send()

    for t in range(chunks):
        for j in range(NZ - 1):
            sum_copy(t, j).wait_send()
            hid_copy(t, j).wait_send()
    unless_own([out_copy(o, tile, n, dc) for o, tile, n in sorted(sum(CHUNKS, ())) for dc in range(NC)])

    total = jnp.zeros(recv_c.shape[1:], F32)
    for chunk in CHUNKS:
        for o, tile, n in chunk:
            for xx in range(NX):
                source = xx * NY + around(y, NY, NY - o)
                here = pl.ds(tile, n)
                pltpu.make_async_copy(
                    send_c.at[0, 0, here], recv_c.at[source, here], crs.at[source, tile]
                ).wait()
    for i in range(NG):
        total = total + recv_c[i].astype(F32)
    total = jnp.concatenate([total[:, :TILE], total[:, TILE:]], axis=2)
    out[...] = total.reshape(out.shape).astype(BF16)


def shards(tokens, gate_weight, up_weight, down_weight):
    rows, kd = tokens.shape
    ff, nd = down_weight.shape
    n, tiles, tall = len(CHUNKS), rows // TILE, NY * TILE
    dma = pltpu.SemaphoreType.DMA
    return pl.pallas_call(
        kernel,
        out_shape=pltpu.VMEM((rows, nd), BF16),
        in_specs=[pl.BlockSpec(memory_space=pl.ANY)] * 4,
        out_specs=pl.BlockSpec(memory_space=pltpu.VMEM),
        scratch_shapes=[
            pltpu.VMEM((rows, kd), BF16),
            pltpu.VMEM((NC * kd, ff), BF16),
            pltpu.VMEM((NC * kd, ff), BF16),
            pltpu.VMEM((NC, ff, nd), BF16),
            pltpu.VMEM((tiles, 2 * TILE, kd // 2), BF16),
            pltpu.VMEM((NY, NC, tiles, 2 * TILE, kd // 2), BF16),
            pltpu.VMEM((n, tall, ff), F32),
            pltpu.VMEM((n, tall, ff), F32),
            pltpu.VMEM((n, NZ - 1, 2 * TILE, ff), BF16),
            pltpu.VMEM((n, NZ - 1, 2 * TILE, ff), BF16),
            pltpu.VMEM((n, NZ, TILE, ff), BF16),
            pltpu.VMEM((NC, tall, nd), F32),
            pltpu.VMEM((NC, NY, tiles, 2 * TILE, nd // 2), BF16),
            pltpu.VMEM((NG, tiles, 2 * TILE, nd // 2), BF16),
            dma((4,)), dma((3,)), dma((3,)),
            dma((NX, NY)), dma((NY, NC)), dma((NY,)), dma((NY,)),
            dma((n, NZ - 1)), dma((n, NZ - 1)), dma((n, NZ - 1)), dma((n, NZ - 1)),
            dma((NC, NY, tiles)), dma((NG, tiles)),
        ],
        compiler_params=pltpu.CompilerParams(collective_id=0, has_side_effects=True, vmem_limit_bytes=60 << 20),
        name="feed_forward",
    )(tokens, gate_weight, up_weight, down_weight)


def solution(mesh):
    in_specs = (P(("depth", "row"), "col"), P("col", "row"), P("col", "row"), P("row", "col"))
    out_specs = P(("depth", "row"), "col")
    return jax.shard_map(shards, mesh=mesh, in_specs=in_specs, out_specs=out_specs, check_vma=False)
```

time: 54.6 us -> 52.8 us (0.967)
  Pallas kernels: 53.8 us -> 52.1 us
    pallas_call x1, Pallas kernels: 53.8 us -> 52.1 us  [shards(): pl.pallas_call(kernel, out_shape=pltpu.VMEM((rows, nd), BF16), in_specs=[...]
where the time goes in v3:
time: 52.8 us; the launch traced here: 52.7 us
  Pallas kernels  52.1 us (99%)
  local copies, waits for them, and re-layouts  0.61 us (1%)
    pallas_call x1, Pallas kernels, shards(): pl.pallas_call(kernel, out_shape=pltpu.VMEM((rows, nd), BF16), in_specs=[...  52.1 us

profile of v3, /device:TPU:1, one launch (start us, length us, event | category | flops | bytes accessed | tf_op | source)
XLA Modules:
  0.0 52.7 jit_solution(17786607612501683148)
XLA Ops:
  0.0 52.1 %feed_forward.1 = bf16[24,512]{1,0:T(8,128)(2,1)S(1)} custom-call(bf16[24,512]{1,0:T(8,128)(2,1)} %tok.1, bf16[512,896]{1,0:T(8,128)(2,1)} %gate.1, bf16[512,896]{1,0:T(8,128)(2,1)} %up.1, bf16[896,512]{1,0:T(8,128)(2,1)} %down.1), custom_call_target="tpu_custom_call" | custom-call | tf_op jit(solution)/shard_map/feed_forward/pallas_call | solution.py:306
  52.1 0.6 %copy.6 = bf16[24,512]{1,0:T(8,128)(2,1)} copy(bf16[24,512]{1,0:T(8,128)(2,1)S(1)} %feed_forward.1) | data formatting | bytes 49152

commit v4 on v3

--- a/solution.py
+++ b/solution.py
@@ -11,7 +11,7 @@
 CHUNKS = (
     ((0, 0, 3), (1, 0, 3), (7, 0, 2)),
     ((4, 0, 3), (3, 0, 3), (5, 0, 2)),
-    ((7, 2, 1), (5, 2, 1), (2, 0, 3), (6, 0, 3)),
+    ((5, 2, 1), (2, 0, 3), (6, 0, 3), (7, 2, 1)),
 )
 DIRECT = tuple((i, i) for i in (4, -3, 3, -2, 2, -1, 1))
 SUM_TREE = (((-1, -4), (-1, -2), (1, 3), (1, 1)), ((-3, -3), (-1, -1), (2, 2)))
@@ -225,9 +225,6 @@
     def down_products(t):
         for j in range(len(HIDS[t][1]), NZ - 1):
             hid_arrived(t, j)
-        if t == 0:
-            loads[2].wait()
-            swaps[2].wait_recv()
         h = hid[t].astype(F32).reshape(NZ * TILE, ff).astype(BF16)
         for cc in range(NC):
             part[cc] = jnp.dot(h, wd[cc], preferred_element_type=F32)
@@ -255,16 +252,17 @@
     up_products(0)
     forward(1)
     forward(2)
-    add_on_way(0)
     up_products(1)
     up_products(2)
     add_on_way(1)
-    hidden(0)
     add_on_way(2)
     hidden(1)
+    hidden(0)
     hidden(2)
+    loads[2].wait()
+    swaps[2].wait_recv()
+    down_products(1)
     down_products(0)
-    down_products(1)
     down_products(2)
 
     for copy in swaps:

time: 52.8 us -> 51.9 us (0.983)
  Pallas kernels: 52.1 us -> 51.1 us
    pallas_call x1, Pallas kernels: 52.1 us -> 51.1 us  [shards(): pl.pallas_call(kernel, out_shape=pltpu.VMEM((rows, nd), BF16), in_specs=[...]
where the time goes in v4:
time: 51.9 us; the launch traced here: 51.8 us
  Pallas kernels  51.1 us (98%)
  local copies, waits for them, and re-layouts  0.61 us (1%)
    pallas_call x1, Pallas kernels, shards(): pl.pallas_call(kernel, out_shape=pltpu.VMEM((rows, nd), BF16), in_specs=[...  51.1 us

profile of v4, /device:TPU:1, one launch (start us, length us, event | category | flops | bytes accessed | tf_op | source)
XLA Modules:
  0.0 51.8 jit_solution(9984601803426466983)
XLA Ops:
  0.0 51.1 %feed_forward.1 = bf16[24,512]{1,0:T(8,128)(2,1)S(1)} custom-call(bf16[24,512]{1,0:T(8,128)(2,1)} %tok.1, bf16[512,896]{1,0:T(8,128)(2,1)} %gate.1, bf16[512,896]{1,0:T(8,128)(2,1)} %up.1, bf16[896,512]{1,0:T(8,128)(2,1)} %down.1), custom_call_target="tpu_custom_call" | custom-call | tf_op jit(solution)/shard_map/feed_forward/pallas_call | solution.py:304
  51.2 0.6 %copy.6 = bf16[24,512]{1,0:T(8,128)(2,1)} copy(bf16[24,512]{1,0:T(8,128)(2,1)S(1)} %feed_forward.1) | data formatting | bytes 49152

commit v5 on v4

--- a/solution.py
+++ b/solution.py
@@ -140,8 +140,8 @@
     tok_sends(0)
     for copy in swaps:
         copy.start()
-    for t in range(1, chunks):
-        tok_sends(t)
+    tok_sends(2)
+    tok_sends(1)
 
     def sum_copy(t, j):
         step = (SUMS[t][0] + SUMS[t][1])[j][0]
@@ -250,8 +250,8 @@
             copy.wait_send()
 
     up_products(0)
+    forward(2)
     forward(1)
-    forward(2)
     up_products(1)
     up_products(2)
     add_on_way(1)

time: 51.9 us -> 53.2 us (1.025)
  Pallas kernels: 51.1 us -> 52.5 us
    pallas_call x1, Pallas kernels: 51.1 us -> 52.5 us  [shards(): pl.pallas_call(kernel, out_shape=pltpu.VMEM((rows, nd), BF16), in_specs=[...]
where the time goes in v5:
time: 53.2 us; the launch traced here: 53.1 us
  Pallas kernels  52.5 us (99%)
  local copies, waits for them, and re-layouts  0.61 us (1%)
    pallas_call x1, Pallas kernels, shards(): pl.pallas_call(kernel, out_shape=pltpu.VMEM((rows, nd), BF16), in_specs=[...  52.5 us

profile of v5, /device:TPU:1, one launch (start us, length us, event | category | flops | bytes accessed | tf_op | source)
XLA Modules:
  0.0 53.1 jit_solution(7386675382612131153)
XLA Ops:
  0.0 52.5 %feed_forward.1 = bf16[24,512]{1,0:T(8,128)(2,1)S(1)} custom-call(bf16[24,512]{1,0:T(8,128)(2,1)} %tok.1, bf16[512,896]{1,0:T(8,128)(2,1)} %gate.1, bf16[512,896]{1,0:T(8,128)(2,1)} %up.1, bf16[896,512]{1,0:T(8,128)(2,1)} %down.1), custom_call_target="tpu_custom_call" | custom-call | tf_op jit(solution)/shard_map/feed_forward/pallas_call | solution.py:304
  52.5 0.6 %copy.6 = bf16[24,512]{1,0:T(8,128)(2,1)} copy(bf16[24,512]{1,0:T(8,128)(2,1)S(1)} %feed_forward.1) | data formatting | bytes 49152
